TPU v7x, 32 devices: a whole 2x2x4 slice. The times are simulated.
32 devices in a mesh: blk: 8 (over y, x, core), rep: 4 (over z).
Axes of the slice: x: 2, y: 2, z: 4, core: 2. Of those that a mesh axis runs over, the one named last changes fastest.
Arguments:
- node_feats: float32 [4096, 256], P('blk'), may hold values from -6 to 6
- operator_tiles: float32 [32, 16, 128, 128], P('blk', 'rep'), may hold values from -0.125 to 0.125
- tile_cols: int32 [32, 16], P('blk', 'rep'), may hold values from 0 to 31, as said below
- weight: float32 [256, 256], replicated, may hold values from -0.375 to 0.375
- layer_bias: float32 [256], replicated, may hold values from -3 to 3
- cotangent: float32 [4096, 256], P(('blk', 'rep')), may hold values from -6 to 6
Outputs:
- layer_out: float32 [4096, 256], P(('blk', 'rep'))
- grad_feats: float32 [4096, 256], P(('blk', 'rep'))
- grad_weight: float32 [256, 256], replicated
- grad_bias: float32 [256], replicated
Inputs may be any that keep to these rules, and one draw needn't show every extreme that they name: `tile_cols`: owner of block j is j // 4, among 8 owners on a closed cycle. Slots r * 4 to (r + 1) * 4 - 1 of row block i name blocks whose owner lies at cycle distance (owner of i minus owner of the column, modulo the number of owners) from r * 2 to (r + 1) * 2 - 1. Slot 0 of row block i names block i itself. Entries may repeat within a row block.
All inputs are finite; a program needn't handle non-finite values.
Results may differ from a plain program's by a relative error of at most 0.0003.
Values sent between devices are 32-bit elements; how exact they have to be, the bound alone decides.
A program may use at most 64 MiB of HBM per device.

v0:
```python
import math

import jax
import jax.numpy as jnp
from jax import lax
from jax.sharding import PartitionSpec as P

TOP_PRECISION = lax.Precision.HIGHEST


def shifted_2(value, axis, steps):
    count = lax.axis_size(axis)
    pairs = [(source, (source + steps) % count) for source in range(count)]
    return lax.ppermute(value, axis, pairs)


def body(node_feats, operator_tiles, tile_cols, weight, layer_bias, cotangent):
    cycle_size = lax.axis_size("blk")
    rep_size = lax.axis_size("rep")
    window = cycle_size // rep_size
    position = lax.axis_index("blk")
    replica = lax.axis_index("rep")
    offset = replica * window
    blocks, slot_count, tile_size, _ = operator_tiles.shape
    width = node_feats.shape[1]
    row_count = blocks * tile_size
    owners = tile_cols // blocks
    within = tile_cols % blocks
    distance = jnp.mod(position - owners, cycle_size) - offset
    columns = jnp.arange(blocks, dtype=jnp.int32)
    sections = jnp.arange(window, dtype=jnp.int32)
    chosen = (
        (distance[:, :, None, None] == sections[None, None, :, None])
        & (within[:, :, None, None] == columns[None, None, None, :])
    ).astype(jnp.float32)

    def reshape_to_blocks(rows):
        return rows.reshape(blocks, tile_size, width)

    def store(stacked, section_no, current):
        return lax.dynamic_update_index_in_dim(stacked, reshape_to_blocks(current), section_no, 0)

    aligned = node_feats
    for bit_pos in range(rep_size.bit_length() - 1):
        shifted = shifted_2(aligned, "blk", window << bit_pos)
        aligned = jnp.where((replica >> bit_pos) % 2 == 1, shifted, aligned)
    empty = jnp.zeros((window, blocks, tile_size, width), jnp.float32)

    def advance(section_no, loop_state):
        current, stacked = loop_state
        current = shifted_2(current, "blk", 1)
        return (current, store(stacked, section_no, current))

    _, received = lax.fori_loop(1, window, advance, (aligned, store(empty, 0, aligned)))
    selected_tiles = jnp.einsum("iksc,scbd->ikbd", chosen, received, precision=TOP_PRECISION)
    partial_aggregate = jnp.einsum(
        "uzrj,uzje->ure", operator_tiles, selected_tiles, precision=TOP_PRECISION
    ).reshape(row_count, width)
    aggregated = lax.psum_scatter(partial_aggregate, "rep", scatter_dimension=0, tiled=True)
    pre_act = jnp.dot(aggregated, weight, precision=TOP_PRECISION) + layer_bias
    negative = jnp.minimum(pre_act, 0.0)
    layer_out = jnp.where(pre_act > 0, pre_act, jnp.expm1(negative))
    grad_pre = cotangent * jnp.where(pre_act > 0, 1.0, jnp.exp(negative))
    grad_scale = 1.0 / math.sqrt(row_count * cycle_size)
    grad_weight = (
        jnp.einsum("rd,re->de", aggregated, grad_pre, precision=TOP_PRECISION) * grad_scale
    )
    grad_bias = jnp.sum(grad_pre, axis=0) * grad_scale
    grad_weight, grad_bias = lax.psum((grad_weight, grad_bias), ("blk", "rep"))
    grad_hidden = jnp.einsum("re,de->rd", grad_pre, weight, precision=TOP_PRECISION)
    hidden_gradient = lax.all_gather(grad_hidden, "rep", axis=0, tiled=True)
    slot_terms = jnp.einsum(
        "xszt,xzc->xstc",
        operator_tiles,
        reshape_to_blocks(hidden_gradient),
        precision=TOP_PRECISION,
    )
    sorted_terms = jnp.einsum("iksc,ikbd->scbd", chosen, slot_terms, precision=TOP_PRECISION)

    def adjoint_term(section_no):
        return lax.dynamic_index_in_dim(sorted_terms, section_no, 0, keepdims=False).reshape(
            row_count, width
        )

    def retreat(counter, running):
        moved = shifted_2(running, "blk", -1)
        return moved + adjoint_term(window - 1 - counter)

    adjoint = lax.fori_loop(1, window, retreat, adjoint_term(window - 1))
    for bit_pos in range(rep_size.bit_length() - 1):
        returned = shifted_2(adjoint, "blk", -(window << bit_pos))
        adjoint = jnp.where((replica >> bit_pos) % 2 == 1, returned, adjoint)
    grad_feats = lax.psum_scatter(adjoint, "rep", scatter_dimension=0, tiled=True)
    return (layer_out, grad_feats, grad_weight, grad_bias)


def solution(mesh):
    return jax.shard_map(
        body,
        mesh=mesh,
        in_specs=(
            P("blk", None),
            P("blk", "rep", None, None),
            P("blk", "rep"),
            P(),
            P(),
            P(("blk", "rep"), None),
        ),
        out_specs=(P(("blk", "rep"), None), P(("blk", "rep"), None), P(), P()),
        check_vma=False,
    )
```

profile of v0, /device:TPU:1, one launch (start us, length us, event | category | flops | bytes accessed | tf_op | source)
XLA Modules:
  0.0 277.3 jit_solution(4873171300348269459)
XLA Ops:
  7.2 2.1 collective-permute-start
  9.3 12.8 %collective-permute-done = f32[512,256]{1,0:T(8,128)S(1)} collective-permute-done((f32[512,256]{1,0:T(8,128)}, f32[512,256]{1,0:T(8,128)S(1)}, u32[]{:S(2)}, u32[]{:S(2)}) %collective-permute-start) | collective-permute-done | bytes 524320 | tf_op jit(solution)/shard_map/ppermute | solution.py:14
  23.3 1.2 collective-permute-start.1
  24.4 11.1 %collective-permute-done.1 = f32[512,256]{1,0:T(8,128)S(1)} collective-permute-done((f32[512,256]{1,0:T(8,128)S(1)}, f32[512,256]{1,0:T(8,128)S(1)}, u32[]{:S(2)}, u32[]{:S(2)}) %collective-permute-start.1) | collective-permute-done | bytes 524320 | tf_op jit(solution)/shard_map/ppermute | solution.py:14
  35.6 2.3 collective-permute-start.2
  37.9 6.1 %collective-permute-done.2 = f32[512,256]{1,0:T(8,128)S(1)} collective-permute-done((f32[512,256]{1,0:T(8,128)S(1)}, f32[512,256]{1,0:T(8,128)S(1)}, u32[]{:S(2)}, u32[]{:S(2)}) %collective-permute-start.2) | collective-permute-done | bytes 524320 | tf_op jit(solution)/shard_map/while/body/eval_jaxpr/ppermute | solution.py:14
  44.1 2.3 fusion.8
  46.4 2.4 fusion.2
  49.0 21.8 %reduce-scatter.3.cloned.1.call-done = f32[128,256]{1,0:T(8,128)} async-done(((f32[512,256]{1,0:T(8,128)}), f32[128,256]{1,0:T(8,128)}) %reduce-scatter.3.cloned.1.call-update) | async-done | bytes 131088 | tf_op jit(solution)/shard_map/reduce_scatter | solution.py:59
  70.8 1.9 fusion.18
  73.1 12.9 %all_gather.3 = f32[512,256]{1,0:T(8,128)S(1)} all-gather(f32[128,256]{1,0:T(8,128)S(1)} %fusion.20), channel_id=1, replica_groups=mesh['blk'=8,'rep'=4] {'rep'}, dimensions={0}, use_global_device_ids=true | all-gather | bytes 655360 | tf_op jit(solution)/shard_map/all_gather | solution.py:71
  86.0 1.9 fusion.23
  87.9 2.1 copy.17
  90.0 4.4 %fusion.5 = f32[2,4,128,256]{3,1,2,0:T(4,128)S(1)} fusion(f32[4,256,4,128]{1,2,0,3:T(4,128)} %copy.17, pred[4,4,4]{1,2,0:T(4,128)(4,1)S(1)} %iota_compare_fusion, pred[4,4,2]{1,0,2:T(4,128)(4,1)S(1)} %iota_compare_fusion.1), kind=kOutput, calls=%fused_computation.5 | convolution fusion | flops 50331776 | bytes 3145824 | tf_op jit(solution)/shard_map/iksc,ikbd->scbd/dot_general | solution.py:78
  94.7 5.4 %collective-permute-start.3 = (f32[512,256]{1,0:T(8,128)S(1)}, f32[512,256]{1,0:T(8,128)S(1)}, u32[]{:S(2)}, u32[]{:S(2)}) collective-permute-start(f32[512,256]{1,0:T(8,128)S(1)} %bitcast.49), channel_id=1, source_target_pairs={{0,28},{4,0},{8,4},{12,8},{16,12},{20,16},{24,20},{28,24},{1,29},{... | collective-permute-start | bytes 1572872 | tf_op jit(solution)/shard_map/while/body/eval_jaxpr/ppermute | solution.py:14
  100.2 7.8 %collective-permute-done.3 = f32[512,256]{1,0:T(8,128)S(1)} collective-permute-done((f32[512,256]{1,0:T(8,128)S(1)}, f32[512,256]{1,0:T(8,128)S(1)}, u32[]{:S(2)}, u32[]{:S(2)}) %collective-permute-start.3) | collective-permute-done | bytes 524320 | tf_op jit(solution)/shard_map/while/body/eval_jaxpr/ppermute | solution.py:14
  108.1 1.3 collective-permute-start.4
  109.3 11.7 %collective-permute-done.4 = f32[512,256]{1,0:T(8,128)S(1)} collective-permute-done((f32[512,256]{1,0:T(8,128)S(1)}, f32[512,256]{1,0:T(8,128)S(1)}, u32[]{:S(2)}, u32[]{:S(2)}) %collective-permute-start.4) | collective-permute-done | bytes 524320 | tf_op jit(solution)/shard_map/ppermute | solution.py:14
  121.1 1.1 collective-permute-start.5
  123.5 11.1 %collective-permute-done.5 = f32[512,256]{1,0:T(8,128)S(1)} collective-permute-done((f32[512,256]{1,0:T(8,128)S(1)}, f32[512,256]{1,0:T(8,128)S(1)}, u32[]{:S(2)}, u32[]{:S(2)}) %collective-permute-start.5) | collective-permute-done | bytes 524320 | tf_op jit(solution)/shard_map/ppermute | solution.py:14
  135.5 39.8 %psum.15 = f32[256]{0:T(256)} all-reduce(f32[256]{0:T(256)S(1)} %broadcast_multiply_fusion), channel_id=1, replica_groups=mesh['blk'=8,'rep'=4] {'blk','rep'}, use_global_device_ids=true, to_apply=%region_4.5 | all-reduce | flops 256 | bytes 2048 | tf_op jit(solution)/shard_map/psum | solution.py:69
  175.3 71.2 %all-reduce.2.cloned.1.call-done = f32[256,256]{1,0:T(8,128)} async-done(((f32[256,256]{1,0:T(8,128)}), f32[256,256]{1,0:T(8,128)}) %all-reduce.2.cloned.1.call-update) | async-done | bytes 262160 | tf_op jit(solution)/shard_map/psum | solution.py:69
  246.5 22.6 %reduce-scatter.5.cloned.1.call-done = f32[128,256]{1,0:T(8,128)} async-done(((f32[512,256]{1,0:T(8,128)}), f32[128,256]{1,0:T(8,128)}) %reduce-scatter.5.cloned.1.call-update) | async-done | bytes 131088 | tf_op jit(solution)/shard_map/reduce_scatter | solution.py:93
  269.1 1.7 copy.29
  (33 shorter events, 4.4 us)
Async XLA Ops:
  7.2 39.2 %copy-start = (f32[4,4,128,128]{3,2,1,0:T(8,128)S(1)}, f32[4,4,128,128]{3,2,1,0:T(8,128)}, u32[]{:S(2)}) copy-start(f32[4,4,128,128]{3,2,1,0:T(8,128)} %param.7) | copy-start | bytes 3145732
  7.2 30.7 %copy-start.4 = (s32[4,4]{1,0:T(4,128)S(1)}, s32[4,4]{1,0:T(4,128)}, u32[]{:S(2)}) copy-start(s32[4,4]{1,0:T(4,128)} %param.8) | copy-start | bytes 196
  7.2 63.6 %reduce-scatter.3.cloned.1.call-start = ((), (), s32[]{:S(2)}) async-start(), calls=%async_computation.2 | async-start | bytes 655360 | tf_op jit(solution)/shard_map/reduce_scatter | solution.py:59
  7.2 14.9 %collective-permute-start = (f32[512,256]{1,0:T(8,128)}, f32[512,256]{1,0:T(8,128)S(1)}, u32[]{:S(2)}, u32[]{:S(2)}) collective-permute-start(f32[512,256]{1,0:T(8,128)} %param.6), channel_id=1, source_target_pairs={{0,8},{4,12},{8,16},{12,20},{16,24},{20,28},{24,0},{28,4},{1,9},{5... | collective-permute-start | bytes 1572872 | tf_op jit(solution)/shard_map/ppermute | solution.py:14
  23.3 12.3 %collective-permute-start.1 = (f32[512,256]{1,0:T(8,128)S(1)}, f32[512,256]{1,0:T(8,128)S(1)}, u32[]{:S(2)}, u32[]{:S(2)}) collective-permute-start(f32[512,256]{1,0:T(8,128)S(1)} %broadcast_select_fusion.1), channel_id=1, source_target_pairs={{0,16},{4,20},{8,24},{12,28},{16,0},{20,4},{24,8},{28,12},{1,17},{... | collective-permute-start | bytes 1572872 | tf_op jit(solution)/shard_map/ppermute | solution.py:14
  35.6 8.4 %collective-permute-start.2 = (f32[512,256]{1,0:T(8,128)S(1)}, f32[512,256]{1,0:T(8,128)S(1)}, u32[]{:S(2)}, u32[]{:S(2)}) collective-permute-start(f32[512,256]{1,0:T(8,128)S(1)} %broadcast_select_fusion.3), channel_id=1, source_target_pairs={{0,4},{4,8},{8,12},{12,16},{16,20},{20,24},{24,28},{28,0},{1,5},{5... | collective-permute-start | bytes 1572872 | tf_op jit(solution)/shard_map/while/body/eval_jaxpr/ppermute | solution.py:14
  46.4 24.4 %copy-start.1 = (f32[128,256]{1,0:T(8,128)S(1)}, f32[128,256]{1,0:T(8,128)}, u32[]{:S(2)}) copy-start(f32[128,256]{1,0:T(8,128)} %param.11) | copy-start | bytes 393220
  46.4 24.4 %copy-start.2 = (f32[256,256]{1,0:T(8,128)S(1)}, f32[256,256]{1,0:T(8,128)}, u32[]{:S(2)}) copy-start(f32[256,256]{1,0:T(8,128)} %param.9) | copy-start | bytes 786436
  46.4 24.4 %copy-start.5 = (f32[256]{0:T(256)S(1)}, f32[256]{0:T(256)}, u32[]{:S(2)}) copy-start(f32[256]{0:T(256)} %param.10) | copy-start | bytes 3076
  48.9 197.6 %all-reduce.2.cloned.1.call-start = ((), (), s32[]{:S(2)}) async-start(), calls=%async_computation.4 | async-start | bytes 524288 | tf_op jit(solution)/shard_map/psum | solution.py:69
  94.7 13.3 %collective-permute-start.3 = (f32[512,256]{1,0:T(8,128)S(1)}, f32[512,256]{1,0:T(8,128)S(1)}, u32[]{:S(2)}, u32[]{:S(2)}) collective-permute-start(f32[512,256]{1,0:T(8,128)S(1)} %bitcast.49), channel_id=1, source_target_pairs={{0,28},{4,0},{8,4},{12,8},{16,12},{20,16},{24,20},{28,24},{1,29},{... | collective-permute-start | bytes 1572872 | tf_op jit(solution)/shard_map/while/body/eval_jaxpr/ppermute | solution.py:14
  100.1 22.2 %copy-start.3 = (f32[128,256]{1,0:T(8,128)S(1)}, f32[128,256]{1,0:T(8,128)}, u32[]{:S(2)}) copy-start(f32[128,256]{1,0:T(8,128)} %reduce-scatter.3.cloned.1.call-done) | copy-start | bytes 393220
  108.1 13.0 %collective-permute-start.4 = (f32[512,256]{1,0:T(8,128)S(1)}, f32[512,256]{1,0:T(8,128)S(1)}, u32[]{:S(2)}, u32[]{:S(2)}) collective-permute-start(f32[512,256]{1,0:T(8,128)S(1)} %bitcast_add_fusion), channel_id=1, source_target_pairs={{0,24},{4,28},{8,0},{12,4},{16,8},{20,12},{24,16},{28,20},{1,25},{... | collective-permute-start | bytes 1572872 | tf_op jit(solution)/shard_map/ppermute | solution.py:14
  121.1 13.4 %collective-permute-start.5 = (f32[512,256]{1,0:T(8,128)S(1)}, f32[512,256]{1,0:T(8,128)S(1)}, u32[]{:S(2)}, u32[]{:S(2)}) collective-permute-start(f32[512,256]{1,0:T(8,128)S(1)} %broadcast_select_fusion), channel_id=1, source_target_pairs={{0,16},{4,20},{8,24},{12,28},{16,0},{20,4},{24,8},{28,12},{1,17},{... | collective-permute-start | bytes 1572872 | tf_op jit(solution)/shard_map/ppermute | solution.py:14
  123.4 145.6 %reduce-scatter.5.cloned.1.call-start = ((), (), s32[]{:S(2)}) async-start(), calls=%async_computation.3 | async-start | bytes 655360 | tf_op jit(solution)/shard_map/reduce_scatter | solution.py:93
Sparse Core Ops, SparseCore 0:
  49.0 21.7 reduce-scatter.2
  123.5 122.9 all-reduce.1
  249.3 19.6 reduce-scatter.4
where the time goes:
time: 280 us; the launch traced here: 277 us
  waiting for transfers between devices  176 us (63%)
  blocking collectives  52.8 us (19%)
  matrix products  14.5 us (5%)
  between operations  13.9 us (5%)
  starting transfers between devices  13.5 us (5%)
  local copies, waits for them, and re-layouts  4.16 us (1%)
    psum x1, waiting for transfers between devices, body(): grad_weight, grad_bias = lax.psum((grad_weight, grad_bias), ('blk', 'rep'))  71.2 us
    ppermute x6, waiting for transfers between devices, shifted_2(): return lax.ppermute(value, axis, pairs)  60.5 us
    psum x1, blocking collectives, body(): grad_weight, grad_bias = lax.psum((grad_weight, grad_bias), ('blk', 'rep'))  39.8 us
    reduce_scatter x1, waiting for transfers between devices, body(): lax.psum_scatter(adjoint, 'rep', scatter_dimension=0, tiled=True)  22.6 us
    reduce_scatter x1, waiting for transfers between devices, body(): lax.psum_scatter(partial_aggregate, 'rep', scatter_dimension=0, tiled=True)  21.8 us
    ppermute x6, starting transfers between devices, shifted_2(): return lax.ppermute(value, axis, pairs)  13.4 us
    all_gather x1, blocking collectives, body(): hidden_gradient = lax.all_gather(grad_hidden, 'rep', axis=0, tiled=True)  12.9 us
  transfers between devices with their start and end apart: 9, of which 9 were waited for; matrix products, arithmetic and copies ran while one was open for 1% of the time, Pallas kernels for 0%

commit v1 on v0

--- a/solution.py
+++ b/solution.py
@@ -1,8 +1,11 @@
+import functools
 import math
 
 import jax
 import jax.numpy as jnp
 from jax import lax
+from jax.experimental import pallas as pl
+from jax.experimental.pallas import tpu as pltpu
 from jax.sharding import PartitionSpec as P
 
 TOP_PRECISION = lax.Precision.HIGHEST
@@ -94,9 +97,303 @@
     return (layer_out, grad_feats, grad_weight, grad_bias)
 
 
+F32, BF16 = jnp.float32, jnp.bfloat16
+HALVES = 2
+
+
+def split(value):
+    high = value.astype(BF16)
+    return high, (value - high.astype(F32)).astype(BF16)
+
+
+def dot3(a, b):
+    def product(x, y):
+        return jnp.dot(x, y, preferred_element_type=F32)
+
+    return product(a[0], b[0]) + (product(a[0], b[1]) + product(a[1], b[0]))
+
+
+def kernel(
+    n, m, feats, tiles, cols, weight, bias, cot,
+    out, gfeats, gweight, gbias,
+    xs, s_hi, s_lo, st_hi, st_lo, hpart, hrecv, grad, adj, fold, total, frecv,
+    gws, gwr, gwz, gfin, send_sem, recv_sem,
+):
+    p, r = lax.axis_index("blk"), lax.axis_index("rep")
+    blocks, slots, size, _ = tiles.shape
+    rows = blocks * size
+    part, width = cot.shape
+    cw = width // HALVES
+    piece = width // n
+    even = lax.rem(p, 2) == 0
+    odd = jnp.logical_not(even)
+    moved = r > 0
+    always = None
+
+    barrier = pltpu.get_barrier_semaphore()
+    for d in range(1, n):
+        pl.semaphore_signal(barrier, inc=1, device_id={"blk": lax.rem(p + d, n), "rep": r})
+    for d in range(1, m):
+        pl.semaphore_signal(barrier, inc=1, device_id={"blk": p, "rep": lax.rem(r + d, m)})
+    pl.semaphore_wait(barrier, n - 1 + m - 1)
+
+    keys, started = {}, []
+
+    def when(cond, action):
+        if cond is None:
+            action()
+        else:
+            pl.when(cond)(action)
+
+    def copy(name, src, dst, blk, rep):
+        key = keys.setdefault(name, len(keys))
+        return pltpu.make_async_remote_copy(
+            src_ref=src,
+            dst_ref=dst,
+            send_sem=send_sem.at[key],
+            recv_sem=recv_sem.at[key],
+            device_id={"blk": blk, "rep": rep},
+        )
+
+    def start(made, cond=always):
+        started.append((made, cond))
+        when(cond, made.start)
+
+    def half(c):
+        return pl.ds(c * cw, cw)
+
+    ahead = lax.rem(p + 2 * r, n)
+    after = lax.rem(p + 2 * r + 1, n)
+    nxt = lax.rem(p + 1, n)
+    first = [copy(("a", c), feats.at[:, half(c)], xs.at[0, c], ahead, r) for c in range(HALVES)]
+    second_odd = [copy(("b", c), feats.at[:, half(c)], xs.at[1, c], after, r) for c in range(HALVES)]
+    second_even = [copy(("b", c), xs.at[0, c], xs.at[1, c], nxt, r) for c in range(HALVES)]
+
+    for c in range(HALVES):
+        start(first[c], moved)
+        start(second_odd[c], odd)
+
+    @pl.when(r == 0)
+    def _():
+        for c in range(HALVES):
+            xs[0, c] = feats[:, half(c)]
+
+    for s in range(2):
+        owner = lax.rem(p - 2 * r - s + 2 * n, n)
+        for b in range(blocks):
+            name = owner * blocks + b
+            at = slice((s * blocks + b) * size, (s * blocks + b + 1) * size)
+            for i in range(blocks):
+                tile = jnp.zeros((size, size), F32)
+                for k in range(slots):
+                    tile = tile + tiles[i, k] * jnp.where(cols[i, k] == name, 1.0, 0.0)
+                high, low = split(tile)
+                s_hi[i * size : (i + 1) * size, at] = high
+                s_lo[i * size : (i + 1) * size, at] = low
+                high, low = split(tile.T)
+                st_hi[at, i * size : (i + 1) * size] = high
+                st_lo[at, i * size : (i + 1) * size] = low
+
+    w = split(weight[...])
+    wt = split(weight[...].T)
+
+    hsends = []
+    for c in range(HALVES):
+        when(moved, first[c].wait_recv)
+        start(second_even[c], even)
+        acc = dot3((s_hi[:, :rows], s_lo[:, :rows]), split(xs[0, c]))
+        second_odd[c].wait_recv()
+        acc = acc + dot3((s_hi[:, rows:], s_lo[:, rows:]), split(xs[1, c]))
+        hpart[c] = acc.reshape(m, part, cw)
+        for d in range(m - 1, 0, -1):
+            to = lax.rem(r + d, m)
+            made = copy(("c", c, d), hpart.at[c, to], hrecv.at[c, d - 1], p, to)
+            start(made)
+            hsends.append(made)
+    for made in hsends:
+        made.wait_recv()
+    agg = jnp.concatenate(
+        [hpart[c, r] + ((hrecv[c, 0] + hrecv[c, 1]) + hrecv[c, 2]) for c in range(HALVES)], axis=1
+    )
+
+    pre = dot3(split(agg), w) + bias[...]
+    exped = jnp.exp(jnp.minimum(pre, 0.0))
+    gpre = cot[...] * jnp.where(pre > 0, 1.0, exped)
+    gpre_parts = split(gpre)
+    gsends = []
+    for c in range(HALVES):
+        columns = slice(c * cw, (c + 1) * cw)
+        grad[c, r] = dot3(gpre_parts, (wt[0][:, columns], wt[1][:, columns]))
+        made_c = []
+        for d in range(m - 1, 0, -1):
+            to = lax.rem(r + d, m)
+            made = copy(("d", c, d), grad.at[c, r], grad.at[c, r], p, to)
+            start(made)
+            made_c.append(made)
+        gsends.append(made_c)
+    out[...] = jnp.where(pre > 0, pre, exped - 1.0)
+
+    gw = dot3(split(agg.T), gpre_parts)
+    gb = jnp.broadcast_to(jnp.sum(gpre, axis=0, keepdims=True), (8, width))
+    for q in range(n):
+        gws[q, :piece] = gw[q * piece : (q + 1) * piece]
+        gws[q, piece:] = gb
+    gwr[p] = gws[p]
+    esends = []
+    for d in range(1, n):
+        to = lax.rem(p + d, n)
+        made = copy(("e", d), gws.at[to], gwr.at[p], to, r)
+        start(made)
+        esends.append(made)
+
+    def weight_sums():
+        for made in esends:
+            made.wait_recv()
+        total_p = gwr[0]
+        for q in range(1, n):
+            total_p = total_p + gwr[q]
+        gwz[r] = total_p
+        made_z = []
+        for d in range(m - 1, 0, -1):
+            to = lax.rem(r + d, m)
+            made = copy(("m", d), gwz.at[r], gwz.at[r], p, to)
+            start(made)
+            made_z.append(made)
+        return made_z
+
+    scale = 1.0 / math.sqrt(rows * n)
+
+    def weight_gather(made_z):
+        for made in made_z:
+            made.wait_recv()
+        whole = gwz[0]
+        for q in range(1, m):
+            whole = whole + gwz[q]
+        gfin[p] = whole[:piece] * scale
+        gbias[...] = whole[piece : piece + 1] * scale
+        made_n = []
+        for d in range(1, n):
+            to = lax.rem(p + d, n)
+            made = copy(("n", d), gfin.at[p], gfin.at[p], to, r)
+            start(made)
+            made_n.append(made)
+        return made_n
+
+    back = lax.rem(p - 2 * r + n, n)
+    before = lax.rem(p - 2 * r - 1 + 2 * n, n)
+    prv = lax.rem(p - 1 + n, n)
+    fold_even = [copy(("f", c), adj.at[1, c], fold.at[c], before, r) for c in range(HALVES)]
+    fold_odd = [copy(("f", c), adj.at[1, c], fold.at[c], prv, r) for c in range(HALVES)]
+    last = [copy(("k", c), adj.at[0, c], total.at[c], back, r) for c in range(HALVES)]
+
+    def adjoint(c):
+        for made in gsends[c]:
+            made.wait_recv()
+        g = split(grad[c].reshape(rows, cw))
+        adj[1, c] = dot3((st_hi[rows:], st_lo[rows:]), g).reshape(m, part, cw)
+        start(fold_odd[c], odd)
+        start(fold_even[c], even)
+        adj[0, c] = dot3((st_hi[:rows], st_lo[:rows]), g).reshape(m, part, cw)
+
+        @pl.when(even)
+        def _():
+            fold_even[c].wait_recv()
+            adj[0, c] = adj[0, c] + fold[c]
+
+        start(last[c], moved)
+
+    def adjoint_reduce(c):
+        when(moved, last[c].wait_recv)
+
+        @pl.when(r == 0)
+        def _():
+            total[c] = adj[0, c]
+
+        @pl.when(odd)
+        def _():
+            fold_even[c].wait_recv()
+            total[c] = total[c] + fold[c]
+
+        made_c = []
+        for d in range(m - 1, 0, -1):
+            to = lax.rem(r + d, m)
+            made = copy(("l", c, d), total.at[c, to], frecv.at[c, d - 1], p, to)
+            start(made)
+            made_c.append(made)
+        return made_c
+
+    adjoint(0)
+    made_z = weight_sums()
+    adjoint(1)
+    lsends = [adjoint_reduce(0)]
+    made_n = weight_gather(made_z)
+    lsends.append(adjoint_reduce(1))
+    for c in range(HALVES):
+        if c == 1:
+            for made in made_n:
+                made.wait_recv()
+            gweight[...] = gfin[...].reshape(width, width)
+        for made in lsends[c]:
+            made.wait_recv()
+        gfeats[:, half(c)] = total[c, r] + ((frecv[c, 0] + frecv[c, 1]) + frecv[c, 2])
+    for made, cond in started:
+        when(cond, made.wait_send)
+
+
+def fast_body(n, m, node_feats, operator_tiles, tile_cols, weight, layer_bias, cotangent):
+    blocks, _, size, _ = operator_tiles.shape
+    rows = blocks * size
+    part, width = cotangent.shape
+    cw = width // HALVES
+    piece = width // n
+    copies = HALVES * (2 + 3 * (m - 1) + 2) + 2 * (n - 1) + (m - 1)
+    vmem = pl.BlockSpec(memory_space=pltpu.VMEM)
+    smem = pl.BlockSpec(memory_space=pltpu.SMEM)
+    shape = jax.ShapeDtypeStruct
+    quarter = (HALVES, m, part, cw)
+    result = pl.pallas_call(
+        functools.partial(kernel, n, m),
+        out_shape=(
+            shape((part, width), F32),
+            shape((part, width), F32),
+            shape((width, width), F32),
+            shape((1, width), F32),
+        ),
+        in_specs=[vmem, vmem, smem, vmem, vmem, vmem],
+        out_specs=(vmem,) * 4,
+        scratch_shapes=[
+            pltpu.VMEM((2, HALVES, rows, cw), F32),
+            pltpu.VMEM((rows, 2 * rows), BF16),
+            pltpu.VMEM((rows, 2 * rows), BF16),
+            pltpu.VMEM((2 * rows, rows), BF16),
+            pltpu.VMEM((2 * rows, rows), BF16),
+            pltpu.VMEM(quarter, F32),
+            pltpu.VMEM((HALVES, m - 1, part, cw), F32),
+            pltpu.VMEM(quarter, F32),
+            pltpu.VMEM((2,) + quarter, F32),
+            pltpu.VMEM(quarter, F32),
+            pltpu.VMEM(quarter, F32),
+            pltpu.VMEM((HALVES, m - 1, part, cw), F32),
+            pltpu.VMEM((n, piece + 8, width), F32),
+            pltpu.VMEM((n, piece + 8, width), F32),
+            pltpu.VMEM((m, piece + 8, width), F32),
+            pltpu.VMEM((n, piece, width), F32),
+            pltpu.SemaphoreType.DMA((copies,)),
+            pltpu.SemaphoreType.DMA((copies,)),
+        ],
+        compiler_params=pltpu.CompilerParams(
+            collective_id=0, has_side_effects=True, vmem_limit_bytes=48 * 1024 * 1024
+        ),
+    )(node_feats, operator_tiles, tile_cols, weight, layer_bias.reshape(1, width), cotangent)
+    layer_out, grad_feats, grad_weight, grad_bias = result
+    return layer_out, grad_feats, grad_weight, grad_bias.reshape(width)
+
+
 def solution(mesh):
+    n, m = mesh.shape["blk"], mesh.shape["rep"]
+    fits = n == 2 * m and m == 4
     return jax.shard_map(
-        body,
+        functools.partial(fast_body, n, m) if fits else body,
         mesh=mesh,
         in_specs=(
             P("blk", None),

time: 280 us -> 72.3 us (0.26)
  the two profiles are of different devices: /device:TPU:1 before, /device:TPU:0 now
where the time goes in v1:
time: 72.3 us; the launch traced here: 72 us
  Pallas kernels  63.3 us (88%)
  local copies, waits for them, and re-layouts  8.05 us (11%)
    pallas_call x1, Pallas kernels, fast_body(): pl.pallas_call(functools.partial(kernel, n, m), out_shape=(shape((part, w...  63.3 us
    unnamed x16, local copies, waits for them, and re-layouts  8.05 us

profile of v1, /device:TPU:0, one launch (start us, length us, event | category | flops | bytes accessed | tf_op | source)
XLA Modules:
  0.0 72.0 jit_solution(9553513909438031576)
XLA Ops:
  0.6 0.0 copy-start.5
  0.6 0.7 copy-done.5
  1.3 0.0 copy-start
  1.3 1.2 %copy-done = f32[4,4,128,128]{3,2,1,0:T(8,128)S(1)} copy-done((f32[4,4,128,128]{3,2,1,0:T(8,128)S(1)}, f32[4,4,128,128]{3,2,1,0:T(8,128)}, u32[]{:S(2)}) %copy-start) | copy-done | bytes 1048600
  2.5 0.0 copy-start.1
  2.5 1.0 %copy-done.1 = f32[512,256]{1,0:T(8,128)S(1)} copy-done((f32[512,256]{1,0:T(8,128)S(1)}, f32[512,256]{1,0:T(8,128)}, u32[]{:S(2)}) %copy-start.1) | copy-done | bytes 524312
  3.6 0.0 copy-start.2
  3.6 0.9 %copy-done.2 = f32[256,256]{1,0:T(8,128)S(1)} copy-done((f32[256,256]{1,0:T(8,128)S(1)}, f32[256,256]{1,0:T(8,128)}, u32[]{:S(2)}) %copy-start.2) | copy-done | bytes 262168
  4.5 0.0 copy-start.3
  4.5 0.9 %copy-done.3 = f32[128,256]{1,0:T(8,128)S(1)} copy-done((f32[128,256]{1,0:T(8,128)S(1)}, f32[128,256]{1,0:T(8,128)}, u32[]{:S(2)}) %copy-start.3) | copy-done | bytes 131096
  5.4 0.0 copy-start.4
  5.4 0.7 copy-done.4
  6.1 63.3 %shard_map.93 = (f32[128,256]{1,0:T(8,128)S(1)}, f32[128,256]{1,0:T(8,128)S(1)}, f32[256,256]{1,0:T(8,128)S(1)}, f32[1,256]{1,0:T(1,128)S(1)}) custom-call(f32[512,256]{1,0:T(8,128)S(1)} %copy-done.1, f32[4,4,128,128]{3,2,1,0:T(8,128)S(1)} %copy-done, s32[4,4]{1,0:T(4,128)S(1)} %copy-done.4, f32[256,256]{1,0:T(8,128)S(1)} %copy-done.2, ...), custom_call_target="tpu_custom_call" | custom-call | tf_op jit(solution)/shard_map/pallas_call | solution.py:354
  69.5 0.7 copy.14
  70.1 0.7 copy.15
  70.8 0.7 copy.16
  71.5 0.6 copy.17
Async XLA Ops:
  0.6 0.7 copy-start.5
  1.3 1.2 %copy-start = (f32[4,4,128,128]{3,2,1,0:T(8,128)S(1)}, f32[4,4,128,128]{3,2,1,0:T(8,128)}, u32[]{:S(2)}) copy-start(f32[4,4,128,128]{3,2,1,0:T(8,128)} %tiles.1) | copy-start | bytes 3145732
  2.5 1.0 %copy-start.1 = (f32[512,256]{1,0:T(8,128)S(1)}, f32[512,256]{1,0:T(8,128)}, u32[]{:S(2)}) copy-start(f32[512,256]{1,0:T(8,128)} %feats.1) | copy-start | bytes 1572868
  3.6 0.9 %copy-start.2 = (f32[256,256]{1,0:T(8,128)S(1)}, f32[256,256]{1,0:T(8,128)}, u32[]{:S(2)}) copy-start(f32[256,256]{1,0:T(8,128)} %weight.1) | copy-start | bytes 786436
  4.5 0.9 %copy-start.3 = (f32[128,256]{1,0:T(8,128)S(1)}, f32[128,256]{1,0:T(8,128)}, u32[]{:S(2)}) copy-start(f32[128,256]{1,0:T(8,128)} %cot.1) | copy-start | bytes 393220
  5.4 0.7 copy-start.4

commit v2 on v1

--- a/solution.py
+++ b/solution.py
@@ -114,10 +114,11 @@
 
 
 def kernel(
-    n, m, feats, tiles, cols, weight, bias, cot,
+    n, m, feats, tiles_hbm, cols_hbm, weight_hbm, bias_hbm, cot_hbm,
     out, gfeats, gweight, gbias,
-    xs, s_hi, s_lo, st_hi, st_lo, hpart, hrecv, grad, adj, fold, total, frecv,
-    gws, gwr, gwz, gfin, send_sem, recv_sem,
+    tiles, cols, weight, bias, cot,
+    xs, s_hi, s_lo, st_hi, st_lo, hpart, hrecv, grad, adj, fold, extra, total, frecv,
+    gws, gwr, gwz, gfin, send_sem, recv_sem, load_sem,
 ):
     p, r = lax.axis_index("blk"), lax.axis_index("rep")
     blocks, slots, size, _ = tiles.shape
@@ -125,25 +126,61 @@
     part, width = cot.shape
     cw = width // HALVES
     piece = width // n
+    kind = lax.rem(p, 4)
     even = lax.rem(p, 2) == 0
     odd = jnp.logical_not(even)
     moved = r > 0
     always = None
+
+    def both(x, y):
+        return jnp.logical_and(x, y)
+
+    def but(x, y):
+        return jnp.logical_and(x, jnp.logical_not(y))
+
+    def when(cond, action):
+        if cond is None:
+            action()
+        else:
+            pl.when(cond)(action)
+
+    near_from = both(r == 1, kind == 2)
+    near_to = both(r == 1, kind == 1)
+    above = both(r == 3, kind == 3)
+    below = both(r == 2, kind == 2)
+    nxt = lax.rem(p + 1, n)
+    prv = lax.rem(p - 1 + n, n)
+
+    pairs = [
+        (tiles_hbm, tiles),
+        (cols_hbm, cols),
+        (weight_hbm, weight),
+        (bias_hbm, bias),
+        (cot_hbm, cot),
+    ]
+    loads = [
+        pltpu.make_async_copy(src, dst, load_sem.at[i]) for i, (src, dst) in enumerate(pairs)
+    ]
+    for made in loads:
+        made.start()
 
     barrier = pltpu.get_barrier_semaphore()
     for d in range(1, n):
         pl.semaphore_signal(barrier, inc=1, device_id={"blk": lax.rem(p + d, n), "rep": r})
     for d in range(1, m):
         pl.semaphore_signal(barrier, inc=1, device_id={"blk": p, "rep": lax.rem(r + d, m)})
-    pl.semaphore_wait(barrier, n - 1 + m - 1)
+
+    @pl.when(above)
+    def _():
+        pl.semaphore_signal(barrier, inc=1, device_id={"blk": prv, "rep": 2})
+
+    @pl.when(below)
+    def _():
+        pl.semaphore_signal(barrier, inc=1, device_id={"blk": nxt, "rep": 3})
+
+    pl.semaphore_wait(barrier, n + m - 2 + jnp.where(jnp.logical_or(above, below), 1, 0))
 
     keys, started = {}, []
-
-    def when(cond, action):
-        if cond is None:
-            action()
-        else:
-            pl.when(cond)(action)
 
     def copy(name, src, dst, blk, rep):
         key = keys.setdefault(name, len(keys))
@@ -164,20 +201,30 @@
 
     ahead = lax.rem(p + 2 * r, n)
     after = lax.rem(p + 2 * r + 1, n)
-    nxt = lax.rem(p + 1, n)
-    first = [copy(("a", c), feats.at[:, half(c)], xs.at[0, c], ahead, r) for c in range(HALVES)]
-    second_odd = [copy(("b", c), feats.at[:, half(c)], xs.at[1, c], after, r) for c in range(HALVES)]
-    second_even = [copy(("b", c), xs.at[0, c], xs.at[1, c], nxt, r) for c in range(HALVES)]
+    to_ahead = but(moved, both(r == 1, lax.rem(ahead, 4) == 1))
+    to_after = but(odd, both(r == 2, lax.rem(after, 4) == 2))
+
+    def to_first(c, src, blk, rep):
+        return copy(("a", c), src, xs.at[0, c], blk, rep)
+
+    def to_second(c, src, blk, rep):
+        return copy(("b", c), src, xs.at[1, c], blk, rep)
 
     for c in range(HALVES):
-        start(first[c], moved)
-        start(second_odd[c], odd)
+        start(to_first(c, feats.at[:, half(c)], ahead, r), to_ahead)
+        start(to_second(c, feats.at[:, half(c)], after, r), to_after)
+    own = [
+        pltpu.make_async_copy(feats.at[:, half(c)], xs.at[0, c], load_sem.at[len(pairs) + c])
+        for c in range(HALVES)
+    ]
 
     @pl.when(r == 0)
     def _():
         for c in range(HALVES):
-            xs[0, c] = feats[:, half(c)]
-
+            own[c].start()
+
+    for made in loads:
+        made.wait()
     for s in range(2):
         owner = lax.rem(p - 2 * r - s + 2 * n, n)
         for b in range(blocks):
@@ -194,28 +241,53 @@
                 st_hi[at, i * size : (i + 1) * size] = high
                 st_lo[at, i * size : (i + 1) * size] = low
 
-    w = split(weight[...])
-    wt = split(weight[...].T)
+    def take_first(c):
+        @pl.when(moved)
+        def _():
+            to_first(c, xs.at[0, c], p, r).wait_recv()
+
+        @pl.when(r == 0)
+        def _():
+            own[c].wait()
+
+        start(to_second(c, xs.at[0, c], nxt, r), even)
+        start(to_second(c, xs.at[0, c], prv, r - 1), above)
+
+    def product(c, s):
+        at = slice(s * rows, (s + 1) * rows)
+        return dot3((s_hi[:, at], s_lo[:, at]), split(xs[s, c]))
 
     hsends = []
-    for c in range(HALVES):
-        when(moved, first[c].wait_recv)
-        start(second_even[c], even)
-        acc = dot3((s_hi[:, :rows], s_lo[:, :rows]), split(xs[0, c]))
-        second_odd[c].wait_recv()
-        acc = acc + dot3((s_hi[:, rows:], s_lo[:, rows:]), split(xs[1, c]))
-        hpart[c] = acc.reshape(m, part, cw)
+
+    def aggregate_sends(c):
         for d in range(m - 1, 0, -1):
             to = lax.rem(r + d, m)
             made = copy(("c", c, d), hpart.at[c, to], hrecv.at[c, d - 1], p, to)
             start(made)
             hsends.append(made)
+
+    for c in range(HALVES):
+        @pl.when(near_from)
+        def _():
+            to_second(c, xs.at[1, c], p, r).wait_recv()
+            to_first(c, xs.at[1, c], prv, r).start()
+
+        take_first(c)
+        acc = product(c, 0)
+        pl.when(jnp.logical_not(near_from))(to_second(c, xs.at[1, c], p, r).wait_recv)
+        acc = acc + product(c, 1)
+        hpart[c] = acc.reshape(m, part, cw)
+        aggregate_sends(c)
+    for c in range(HALVES):
+        started.append((to_first(c, xs.at[1, c], prv, r), near_from))
     for made in hsends:
         made.wait_recv()
     agg = jnp.concatenate(
         [hpart[c, r] + ((hrecv[c, 0] + hrecv[c, 1]) + hrecv[c, 2]) for c in range(HALVES)], axis=1
     )
 
+    w = split(weight[...])
+    wt = split(weight[...].T)
     pre = dot3(split(agg), w) + bias[...]
     exped = jnp.exp(jnp.minimum(pre, 0.0))
     gpre = cot[...] * jnp.where(pre > 0, 1.0, exped)
@@ -281,45 +353,109 @@
 
     back = lax.rem(p - 2 * r + n, n)
     before = lax.rem(p - 2 * r - 1 + 2 * n, n)
-    prv = lax.rem(p - 1 + n, n)
-    fold_even = [copy(("f", c), adj.at[1, c], fold.at[c], before, r) for c in range(HALVES)]
-    fold_odd = [copy(("f", c), adj.at[1, c], fold.at[c], prv, r) for c in range(HALVES)]
-    last = [copy(("k", c), adj.at[0, c], total.at[c], back, r) for c in range(HALVES)]
+    order = [m - 1 - j for j in range(m)]
+
+    def place(d):
+        return lax.rem(r + d, m)
+
+    def to_fold(c, d, blk):
+        b = place(d)
+        return copy(("f", c, d), adj.at[1, c, b], fold.at[c, b], blk, r)
+
+    def to_near(c, d):
+        b = place(d)
+        return copy(("g", c, d), adj.at[0, c, b], extra.at[c, b], nxt, r)
+
+    def to_above(c, b):
+        return copy(("h", c, b), adj.at[1, c, b], extra.at[c, b], nxt, r + 1)
+
+    def to_total(c, d):
+        b = place(d)
+        return copy(("k", c, d), adj.at[0, c, b], total.at[c, b], back, r)
+
+    plain_second = but(but(even, below), near_from)
+    plain_first = but(but(both(odd, moved), near_to), above)
 
     def adjoint(c):
         for made in gsends[c]:
             made.wait_recv()
         g = split(grad[c].reshape(rows, cw))
         adj[1, c] = dot3((st_hi[rows:], st_lo[rows:]), g).reshape(m, part, cw)
-        start(fold_odd[c], odd)
-        start(fold_even[c], even)
+        for d in order:
+            start(to_fold(c, d, prv), odd)
+            start(to_fold(c, d, before), plain_second)
+        for b in range(m):
+            start(to_above(c, b), below)
         adj[0, c] = dot3((st_hi[:rows], st_lo[:rows]), g).reshape(m, part, cw)
+        for d in order:
+            start(to_near(c, d), near_to)
+            start(to_total(c, d), plain_first)
 
         @pl.when(even)
         def _():
-            fold_even[c].wait_recv()
-            adj[0, c] = adj[0, c] + fold[c]
-
-        start(last[c], moved)
+            for d in order:
+                b = place(d)
+                to_fold(c, d, prv).wait_recv()
+                adj[0, c, b] = adj[0, c, b] + fold[c, b]
+                pl.when(moved)(to_total(c, d).start)
+
+        @pl.when(above)
+        def _():
+            for d in order:
+                b = (3 + d) % m
+                to_above(c, b).wait_recv()
+                adj[0, c, b] = adj[0, c, b] + extra[c, b]
+                to_total(c, d).start()
+
+        @pl.when(near_from)
+        def _():
+            for d in order:
+                b = place(d)
+                to_near(c, d).wait_recv()
+                adj[1, c, b] = adj[1, c, b] + extra[c, b]
+                to_fold(c, d, before).start()
+
+        for d in order:
+            started.append((to_total(c, d), both(even, moved)))
+            started.append((to_total(c, d), above))
+            started.append((to_fold(c, d, before), near_from))
+
+    from_total = but(moved, both(r == 1, kind == 3))
+    from_fold = but(odd, both(r == 2, kind == 1))
 
     def adjoint_reduce(c):
-        when(moved, last[c].wait_recv)
-
-        @pl.when(r == 0)
-        def _():
-            total[c] = adj[0, c]
-
-        @pl.when(odd)
-        def _():
-            fold_even[c].wait_recv()
-            total[c] = total[c] + fold[c]
-
         made_c = []
-        for d in range(m - 1, 0, -1):
-            to = lax.rem(r + d, m)
-            made = copy(("l", c, d), total.at[c, to], frecv.at[c, d - 1], p, to)
-            start(made)
-            made_c.append(made)
+        for d in order:
+            b = place(d)
+
+            @pl.when(from_total)
+            def _():
+                to_total(c, d).wait_recv()
+
+            @pl.when(r == 0)
+            def _():
+                total[c, b] = adj[0, c, b]
+
+            @pl.when(from_fold)
+            def _():
+                to_fold(c, d, prv).wait_recv()
+
+                @pl.when(from_total)
+                def _():
+                    total[c, b] = total[c, b] + fold[c, b]
+
+                @pl.when(r == 0)
+                def _():
+                    total[c, b] = total[c, b] + fold[c, b]
+
+                @pl.when(both(r == 1, kind == 3))
+                def _():
+                    total[c, b] = fold[c, b]
+
+            if d:
+                made = copy(("l", c, d), total.at[c, b], frecv.at[c, d - 1], p, b)
+                start(made)
+                made_c.append(made)
         return made_c
 
     adjoint(0)
@@ -346,9 +482,8 @@
     part, width = cotangent.shape
     cw = width // HALVES
     piece = width // n
-    copies = HALVES * (2 + 3 * (m - 1) + 2) + 2 * (n - 1) + (m - 1)
+    copies = HALVES * (2 + 3 * (m - 1) + 4 * m) + 2 * (n - 1) + (m - 1)
     vmem = pl.BlockSpec(memory_space=pltpu.VMEM)
-    smem = pl.BlockSpec(memory_space=pltpu.SMEM)
     shape = jax.ShapeDtypeStruct
     quarter = (HALVES, m, part, cw)
     result = pl.pallas_call(
@@ -359,9 +494,14 @@
             shape((width, width), F32),
             shape((1, width), F32),
         ),
-        in_specs=[vmem, vmem, smem, vmem, vmem, vmem],
+        in_specs=[pl.BlockSpec(memory_space=pltpu.HBM)] * 6,
         out_specs=(vmem,) * 4,
         scratch_shapes=[
+            pltpu.VMEM(operator_tiles.shape, F32),
+            pltpu.SMEM(tile_cols.shape, jnp.int32),
+            pltpu.VMEM((width, width), F32),
+            pltpu.VMEM((1, width), F32),
+            pltpu.VMEM((part, width), F32),
             pltpu.VMEM((2, HALVES, rows, cw), F32),
             pltpu.VMEM((rows, 2 * rows), BF16),
             pltpu.VMEM((rows, 2 * rows), BF16),
@@ -373,6 +513,7 @@
             pltpu.VMEM((2,) + quarter, F32),
             pltpu.VMEM(quarter, F32),
             pltpu.VMEM(quarter, F32),
+            pltpu.VMEM(quarter, F32),
             pltpu.VMEM((HALVES, m - 1, part, cw), F32),
             pltpu.VMEM((n, piece + 8, width), F32),
             pltpu.VMEM((n, piece + 8, width), F32),
@@ -380,9 +521,10 @@
             pltpu.VMEM((n, piece, width), F32),
             pltpu.SemaphoreType.DMA((copies,)),
             pltpu.SemaphoreType.DMA((copies,)),
+            pltpu.SemaphoreType.DMA((5 + HALVES,)),
         ],
         compiler_params=pltpu.CompilerParams(
-            collective_id=0, has_side_effects=True, vmem_limit_bytes=48 * 1024 * 1024
+            collective_id=0, has_side_effects=True, vmem_limit_bytes=63 * 1024 * 1024
         ),
     )(node_feats, operator_tiles, tile_cols, weight, layer_bias.reshape(1, width), cotangent)
     layer_out, grad_feats, grad_weight, grad_bias = result

time: 72.3 us -> 70.7 us (0.978)
  the two profiles are of different devices: /device:TPU:0 before, /device:TPU:1 now
where the time goes in v2:
time: 70.7 us; the launch traced here: 70.5 us
  Pallas kernels  66.3 us (94%)
  local copies, waits for them, and re-layouts  3.55 us (5%)
    pallas_call x1, Pallas kernels, fast_body(): pl.pallas_call(functools.partial(kernel, n, m), out_shape=(shape((part, w...  66.3 us
    unnamed x10, local copies, waits for them, and re-layouts  3.55 us

profile of v2, /device:TPU:1, one launch (start us, length us, event | category | flops | bytes accessed | tf_op | source)
XLA Modules:
  0.0 70.5 jit_solution(10288366145662344883)
XLA Ops:
  0.6 66.3 %shard_map.93 = (f32[128,256]{1,0:T(8,128)}, f32[128,256]{1,0:T(8,128)}, f32[256,256]{1,0:T(8,128)}, f32[1,256]{1,0:T(1,128)}) custom-call(f32[512,256]{1,0:T(8,128)} %feats.1, f32[4,4,128,128]{3,2,1,0:T(8,128)} %tiles_hbm.1, s32[4,4]{1,0:T(4,128)} %cols_hbm.1, f32[256,256]{1,0:T(8,128)} %weight_hbm.1, f32[1,256]{1,0:T(1,128)} %bitcast.2, f32[128,256]{1,0:T(8,128)} %cot_hbm.1), custom_call_target="tpu_custom_call" | custom-call | tf_op jit(solution)/shard_map/pallas_call | solution.py:489
  67.0 0.0 copy-start.1
  67.0 0.0 copy-start
  67.0 1.6 %copy.14 = f32[128,256]{1,0:T(8,128)} copy(f32[128,256]{1,0:T(8,128)} %get-tuple-element.16) | data formatting | bytes 262144
  68.6 0.0 copy-done.1
  68.6 0.7 copy.15
  69.3 0.0 copy-done
  69.3 0.0 copy-start.2
  69.3 0.7 copy.16
  70.0 0.0 copy-done.2
  70.0 0.6 copy.17
Async XLA Ops:
  67.0 1.6 %copy-start.1 = (f32[128,256]{1,0:T(8,128)S(1)}, f32[128,256]{1,0:T(8,128)}, u32[]{:S(2)}) copy-start(f32[128,256]{1,0:T(8,128)} %get-tuple-element.17) | copy-start | bytes 393220
  67.0 2.3 %copy-start = (f32[256,256]{1,0:T(8,128)S(1)}, f32[256,256]{1,0:T(8,128)}, u32[]{:S(2)}) copy-start(f32[256,256]{1,0:T(8,128)} %get-tuple-element.18) | copy-start | bytes 786436
  69.3 0.7 %copy-start.2 = (f32[1,256]{1,0:T(1,128)S(1)}, f32[1,256]{1,0:T(1,128)}, u32[]{:S(2)}) copy-start(f32[1,256]{1,0:T(1,128)} %get-tuple-element.11) | copy-start | bytes 3076

commit v3 on v2

--- a/solution.py
+++ b/solution.py
@@ -210,9 +210,13 @@
     def to_second(c, src, blk, rep):
         return copy(("b", c), src, xs.at[1, c], blk, rep)
 
-    for c in range(HALVES):
+    def send_features(c):
+        start(to_second(c, feats.at[:, half(c)], after, r), to_after)
         start(to_first(c, feats.at[:, half(c)], ahead, r), to_ahead)
-        start(to_second(c, feats.at[:, half(c)], after, r), to_after)
+
+    send_features(0)
+    features_out = list(started)
+    started.clear()
     own = [
         pltpu.make_async_copy(feats.at[:, half(c)], xs.at[0, c], load_sem.at[len(pairs) + c])
         for c in range(HALVES)
@@ -226,6 +230,10 @@
     for made in loads:
         made.wait()
     for s in range(2):
+        if s == 1:
+            for made, cond in features_out:
+                when(cond, made.wait_send)
+            send_features(1)
         owner = lax.rem(p - 2 * r - s + 2 * n, n)
         for b in range(blocks):
             name = owner * blocks + b
@@ -260,11 +268,13 @@
     hsends = []
 
     def aggregate_sends(c):
+        made_c = []
         for d in range(m - 1, 0, -1):
             to = lax.rem(r + d, m)
             made = copy(("c", c, d), hpart.at[c, to], hrecv.at[c, d - 1], p, to)
             start(made)
-            hsends.append(made)
+            made_c.append(made)
+        hsends.append(made_c)
 
     for c in range(HALVES):
         @pl.when(near_from)
@@ -280,29 +290,37 @@
         aggregate_sends(c)
     for c in range(HALVES):
         started.append((to_first(c, xs.at[1, c], prv, r), near_from))
-    for made in hsends:
-        made.wait_recv()
-    agg = jnp.concatenate(
-        [hpart[c, r] + ((hrecv[c, 0] + hrecv[c, 1]) + hrecv[c, 2]) for c in range(HALVES)], axis=1
-    )
-
     w = split(weight[...])
     wt = split(weight[...].T)
-    pre = dot3(split(agg), w) + bias[...]
+    pre = bias[...]
+    parts = []
+    for c in range(HALVES):
+        for made in hsends[c]:
+            made.wait_recv()
+        parts.append(hpart[c, r] + ((hrecv[c, 0] + hrecv[c, 1]) + hrecv[c, 2]))
+        inner = slice(c * cw, (c + 1) * cw)
+        pre = pre + dot3(split(parts[c]), (w[0][inner], w[1][inner]))
+    agg = jnp.concatenate(parts, axis=1)
+
     exped = jnp.exp(jnp.minimum(pre, 0.0))
     gpre = cot[...] * jnp.where(pre > 0, 1.0, exped)
     gpre_parts = split(gpre)
     gsends = []
-    for c in range(HALVES):
-        columns = slice(c * cw, (c + 1) * cw)
-        grad[c, r] = dot3(gpre_parts, (wt[0][:, columns], wt[1][:, columns]))
+
+    def hidden_sends(c):
         made_c = []
         for d in range(m - 1, 0, -1):
             to = lax.rem(r + d, m)
             made = copy(("d", c, d), grad.at[c, r], grad.at[c, r], p, to)
-            start(made)
+            made.start()
             made_c.append(made)
         gsends.append(made_c)
+
+    for c in range(HALVES):
+        columns = slice(c * cw, (c + 1) * cw)
+        grad[c, r] = dot3(gpre_parts, (wt[0][:, columns], wt[1][:, columns]))
+        if c == 0:
+            hidden_sends(0)
     out[...] = jnp.where(pre > 0, pre, exped - 1.0)
 
     gw = dot3(split(agg.T), gpre_parts)
@@ -458,6 +476,11 @@
                 made_c.append(made)
         return made_c
 
+    for made in gsends[0]:
+        made.wait_send()
+    hidden_sends(1)
+    for made in gsends[1]:
+        started.append((made, always))
     adjoint(0)
     made_z = weight_sums()
     adjoint(1)
@@ -474,6 +497,16 @@
         gfeats[:, half(c)] = total[c, r] + ((frecv[c, 0] + frecv[c, 1]) + frecv[c, 2])
     for made, cond in started:
         when(cond, made.wait_send)
+
+
+def store_results(*refs):
+    count = len(refs) // 2
+    sems = refs[-1]
+    copies = [pltpu.make_async_copy(refs[i], refs[count + i], sems.at[i]) for i in range(count)]
+    for made in copies:
+        made.start()
+    for made in copies:
+        made.wait()
 
 
 def fast_body(n, m, node_feats, operator_tiles, tile_cols, weight, layer_bias, cotangent):
@@ -527,7 +560,13 @@
             collective_id=0, has_side_effects=True, vmem_limit_bytes=63 * 1024 * 1024
         ),
     )(node_feats, operator_tiles, tile_cols, weight, layer_bias.reshape(1, width), cotangent)
-    layer_out, grad_feats, grad_weight, grad_bias = result
+    layer_out, grad_feats, grad_weight, grad_bias = pl.pallas_call(
+        store_results,
+        out_shape=[shape(value.shape, F32) for value in result],
+        in_specs=[pl.BlockSpec(memory_space=pl.ANY)] * len(result),
+        out_specs=[pl.BlockSpec(memory_space=pl.ANY)] * len(result),
+        scratch_shapes=[pltpu.SemaphoreType.DMA((len(result),))],
+    )(*result)
     return layer_out, grad_feats, grad_weight, grad_bias.reshape(width)
 
 

time: 70.7 us -> 83 us (1.17)
  Pallas kernels: 66.3 us -> 82.2 us
  local copies, waits for them, and re-layouts: 3.55 us -> 0 us
    pallas_call x0 -> x1, Pallas kernels: none -> 17.1 us  [fast_body(): pl.pallas_call(store_results, out_shape=[shape(value.shape, F32) for valu...]
    unnamed x10 -> x0, local copies, waits for them, and re-layouts: 3.55 us -> none
    pallas_call x1, Pallas kernels: 66.3 us -> 65.1 us  [fast_body(): pl.pallas_call(functools.partial(kernel, n, m), out_shape=(shape((part, w...]
where the time goes in v3:
time: 83 us; the launch traced here: 82.8 us
  Pallas kernels  82.2 us (99%)
    pallas_call x1, Pallas kernels, fast_body(): pl.pallas_call(functools.partial(kernel, n, m), out_shape=(shape((part, w...  65.1 us
    pallas_call x1, Pallas kernels, fast_body(): pl.pallas_call(store_results, out_shape=[shape(value.shape, F32) for valu...  17.1 us

profile of v3, /device:TPU:1, one launch (start us, length us, event | category | flops | bytes accessed | tf_op | source)
XLA Modules:
  0.0 82.8 jit_solution(2682960658091539398)
XLA Ops:
  0.6 65.1 %shard_map.93 = (f32[128,256]{1,0:T(8,128)}, f32[128,256]{1,0:T(8,128)}, f32[256,256]{1,0:T(8,128)}, f32[1,256]{1,0:T(1,128)}) custom-call(f32[512,256]{1,0:T(8,128)} %feats.1, f32[4,4,128,128]{3,2,1,0:T(8,128)} %tiles_hbm.1, s32[4,4]{1,0:T(4,128)} %cols_hbm.1, f32[256,256]{1,0:T(8,128)} %weight_hbm.1, f32[1,256]{1,0:T(1,128)} %bitcast.2, f32[128,256]{1,0:T(8,128)} %cot_hbm.1), custom_call_target="tpu_custom_call" | custom-call | tf_op jit(solution)/shard_map/pallas_call | solution.py:522
  65.8 17.1 %shard_map.94 = (f32[128,256]{1,0:T(8,128)}, f32[128,256]{1,0:T(8,128)}, f32[256,256]{1,0:T(8,128)}, f32[1,256]{1,0:T(1,128)}) custom-call(f32[128,256]{1,0:T(8,128)} %get-tuple-element.12.refs_0_, f32[128,256]{1,0:T(8,128)} %get-tuple-element.13.refs_1_, f32[256,256]{1,0:T(8,128)} %get-tuple-element.14.refs_2_, f32[1,256]{1,0:T(1,128)} %get-tuple-element.15.refs_3_), custom_call_target="tpu_custom_call" | custom-call | tf_op jit(solution)/shard_map/pallas_call | solution.py:563

commit v4 on v3

--- a/solution.py
+++ b/solution.py
@@ -196,13 +196,17 @@
         started.append((made, cond))
         when(cond, made.start)
 
+    def flush():
+        for made, cond in started:
+            when(cond, made.wait_send)
+        started.clear()
+
     def half(c):
         return pl.ds(c * cw, cw)
 
     ahead = lax.rem(p + 2 * r, n)
     after = lax.rem(p + 2 * r + 1, n)
-    to_ahead = but(moved, both(r == 1, lax.rem(ahead, 4) == 1))
-    to_after = but(odd, both(r == 2, lax.rem(after, 4) == 2))
+    to_ahead, to_after = moved, odd
 
     def to_first(c, src, blk, rep):
         return copy(("a", c), src, xs.at[0, c], blk, rep)
@@ -215,8 +219,6 @@
         start(to_first(c, feats.at[:, half(c)], ahead, r), to_ahead)
 
     send_features(0)
-    features_out = list(started)
-    started.clear()
     own = [
         pltpu.make_async_copy(feats.at[:, half(c)], xs.at[0, c], load_sem.at[len(pairs) + c])
         for c in range(HALVES)
@@ -231,8 +233,7 @@
         made.wait()
     for s in range(2):
         if s == 1:
-            for made, cond in features_out:
-                when(cond, made.wait_send)
+            flush()
             send_features(1)
         owner = lax.rem(p - 2 * r - s + 2 * n, n)
         for b in range(blocks):
@@ -259,7 +260,6 @@
             own[c].wait()
 
         start(to_second(c, xs.at[0, c], nxt, r), even)
-        start(to_second(c, xs.at[0, c], prv, r - 1), above)
 
     def product(c, s):
         at = slice(s * rows, (s + 1) * rows)
@@ -277,19 +277,12 @@
         hsends.append(made_c)
 
     for c in range(HALVES):
-        @pl.when(near_from)
-        def _():
-            to_second(c, xs.at[1, c], p, r).wait_recv()
-            to_first(c, xs.at[1, c], prv, r).start()
-
         take_first(c)
         acc = product(c, 0)
-        pl.when(jnp.logical_not(near_from))(to_second(c, xs.at[1, c], p, r).wait_recv)
+        to_second(c, xs.at[1, c], p, r).wait_recv()
         acc = acc + product(c, 1)
         hpart[c] = acc.reshape(m, part, cw)
         aggregate_sends(c)
-    for c in range(HALVES):
-        started.append((to_first(c, xs.at[1, c], prv, r), near_from))
     w = split(weight[...])
     wt = split(weight[...].T)
     pre = bias[...]
@@ -479,6 +472,7 @@
     for made in gsends[0]:
         made.wait_send()
     hidden_sends(1)
+    flush()
     for made in gsends[1]:
         started.append((made, always))
     adjoint(0)
@@ -487,6 +481,7 @@
     lsends = [adjoint_reduce(0)]
     made_n = weight_gather(made_z)
     lsends.append(adjoint_reduce(1))
+    flush()
     for c in range(HALVES):
         if c == 1:
             for made in made_n:
@@ -495,17 +490,25 @@
         for made in lsends[c]:
             made.wait_recv()
         gfeats[:, half(c)] = total[c, r] + ((frecv[c, 0] + frecv[c, 1]) + frecv[c, 2])
-    for made, cond in started:
-        when(cond, made.wait_send)
+    flush()
 
 
 def store_results(*refs):
-    count = len(refs) // 2
+    count = len(refs) // 3
+    sources, targets, stages = refs[:count], refs[count : 2 * count], refs[2 * count : 3 * count]
     sems = refs[-1]
-    copies = [pltpu.make_async_copy(refs[i], refs[count + i], sems.at[i]) for i in range(count)]
-    for made in copies:
+    loads = [
+        pltpu.make_async_copy(sources[i], stages[i], sems.at[0, i]) for i in range(count)
+    ]
+    stores = [
+        pltpu.make_async_copy(stages[i], targets[i], sems.at[1, i]) for i in range(count)
+    ]
+    for made in loads:
         made.start()
-    for made in copies:
+    for load, store in zip(loads, stores):
+        load.wait()
+        store.start()
+    for made in stores:
         made.wait()
 
 
@@ -565,7 +568,9 @@
         out_shape=[shape(value.shape, F32) for value in result],
         in_specs=[pl.BlockSpec(memory_space=pl.ANY)] * len(result),
         out_specs=[pl.BlockSpec(memory_space=pl.ANY)] * len(result),
-        scratch_shapes=[pltpu.SemaphoreType.DMA((len(result),))],
+        scratch_shapes=[pltpu.VMEM(value.shape, F32) for value in result]
+        + [pltpu.SemaphoreType.DMA((2, len(result)))],
+        compiler_params=pltpu.CompilerParams(vmem_limit_bytes=63 * 1024 * 1024),
     )(*result)
     return layer_out, grad_feats, grad_weight, grad_bias.reshape(width)
 

time: 83 us -> 67.7 us (0.82)
  Pallas kernels: 82.2 us -> 66.9 us
    pallas_call x1, Pallas kernels: 17.1 us -> 1.86 us  [fast_body(): pl.pallas_call(store_results, out_shape=[shape(value.shape, F32) for valu...]
where the time goes in v4:
time: 67.7 us; the launch traced here: 67.6 us
  Pallas kernels  66.9 us (99%)
    pallas_call x1, Pallas kernels, fast_body(): pl.pallas_call(functools.partial(kernel, n, m), out_shape=(shape((part, w...  65.1 us
    pallas_call x1, Pallas kernels, fast_body(): pl.pallas_call(store_results, out_shape=[shape(value.shape, F32) for valu...  1.86 us

profile of v4, /device:TPU:1, one launch (start us, length us, event | category | flops | bytes accessed | tf_op | source)
XLA Modules:
  0.0 67.6 jit_solution(10871144884878827842)
XLA Ops:
  0.6 65.1 %shard_map.93 = (f32[128,256]{1,0:T(8,128)}, f32[128,256]{1,0:T(8,128)}, f32[256,256]{1,0:T(8,128)}, f32[1,256]{1,0:T(1,128)}) custom-call(f32[512,256]{1,0:T(8,128)} %feats.1, f32[4,4,128,128]{3,2,1,0:T(8,128)} %tiles_hbm.1, s32[4,4]{1,0:T(4,128)} %cols_hbm.1, f32[256,256]{1,0:T(8,128)} %weight_hbm.1, f32[1,256]{1,0:T(1,128)} %bitcast.2, f32[128,256]{1,0:T(8,128)} %cot_hbm.1), custom_call_target="tpu_custom_call" | custom-call | tf_op jit(solution)/shard_map/pallas_call | solution.py:525
  65.7 1.9 %shard_map.94 = (f32[128,256]{1,0:T(8,128)}, f32[128,256]{1,0:T(8,128)}, f32[256,256]{1,0:T(8,128)}, f32[1,256]{1,0:T(1,128)}) custom-call(f32[128,256]{1,0:T(8,128)} %get-tuple-element.12.refs_0_, f32[128,256]{1,0:T(8,128)} %get-tuple-element.13.refs_1_, f32[256,256]{1,0:T(8,128)} %get-tuple-element.14.refs_2_, f32[1,256]{1,0:T(1,128)} %get-tuple-element.15.refs_3_), custom_call_target="tpu_custom_call" | custom-call | tf_op jit(solution)/shard_map/pallas_call | solution.py:566

commit v5 on v4

--- a/solution.py
+++ b/solution.py
@@ -99,6 +99,7 @@
 
 F32, BF16 = jnp.float32, jnp.bfloat16
 HALVES = 2
+ROW_PARTS = 2
 
 
 def split(value):
@@ -267,14 +268,24 @@
 
     hsends = []
 
+    some = part // ROW_PARTS
+
+    def row_part(s):
+        return pl.ds(s * some, some)
+
     def aggregate_sends(c):
-        made_c = []
-        for d in range(m - 1, 0, -1):
-            to = lax.rem(r + d, m)
-            made = copy(("c", c, d), hpart.at[c, to], hrecv.at[c, d - 1], p, to)
-            start(made)
-            made_c.append(made)
-        hsends.append(made_c)
+        last_half = c == HALVES - 1
+        spans = [row_part(s) for s in range(ROW_PARTS)] if last_half else [pl.ds(0, part)]
+        for s, span in enumerate(spans):
+            made_s = []
+            for d in range(m - 1, 0, -1):
+                to = lax.rem(r + d, m)
+                made = copy(
+                    ("c", c, s, d), hpart.at[c, to, span], hrecv.at[c, d - 1, span], p, to
+                )
+                start(made)
+                made_s.append(made)
+            hsends.append(made_s)
 
     for c in range(HALVES):
         take_first(c)
@@ -285,36 +296,55 @@
         aggregate_sends(c)
     w = split(weight[...])
     wt = split(weight[...].T)
-    pre = bias[...]
-    parts = []
-    for c in range(HALVES):
-        for made in hsends[c]:
+
+    def aggregate(c, span):
+        received = (hrecv[c, 0, span] + hrecv[c, 1, span]) + hrecv[c, 2, span]
+        return hpart[c, r, span] + received
+
+    def times_weight(value, c):
+        inner = slice(c * cw, (c + 1) * cw)
+        return dot3(split(value), (w[0][inner], w[1][inner]))
+
+    for made in hsends[0]:
+        made.wait_recv()
+    early = aggregate(0, pl.ds(0, part))
+    early_pre = times_weight(early, 0) + bias[...]
+
+    forward = list(started)
+    started.clear()
+
+    gsends = [[] for _ in range(HALVES)]
+    aggs, gpres = [], []
+    for s in range(ROW_PARTS):
+        here = slice(s * some, (s + 1) * some)
+        for made in hsends[1 + s]:
             made.wait_recv()
-        parts.append(hpart[c, r] + ((hrecv[c, 0] + hrecv[c, 1]) + hrecv[c, 2]))
-        inner = slice(c * cw, (c + 1) * cw)
-        pre = pre + dot3(split(parts[c]), (w[0][inner], w[1][inner]))
-    agg = jnp.concatenate(parts, axis=1)
-
-    exped = jnp.exp(jnp.minimum(pre, 0.0))
-    gpre = cot[...] * jnp.where(pre > 0, 1.0, exped)
+        late = aggregate(1, row_part(s))
+        pre = early_pre[here] + times_weight(late, 1)
+        exped = jnp.exp(jnp.minimum(pre, 0.0))
+        gpre = cot[here] * jnp.where(pre > 0, 1.0, exped)
+        gpre_parts = split(gpre)
+        for c in range(HALVES):
+            columns = slice(c * cw, (c + 1) * cw)
+            grad[c, r, row_part(s)] = dot3(gpre_parts, (wt[0][:, columns], wt[1][:, columns]))
+            if c == 0:
+                for d in range(m - 1, 0, -1):
+                    to = lax.rem(r + d, m)
+                    block = grad.at[c, r, row_part(s)]
+                    made = copy(("d", c, s, d), block, block, p, to)
+                    start(made)
+                    gsends[c].append(made)
+        out[here] = jnp.where(pre > 0, pre, exped - 1.0)
+        aggs.append(jnp.concatenate([early[here], late], axis=1))
+        gpres.append(gpre)
+    for d in range(m - 1, 0, -1):
+        to = lax.rem(r + d, m)
+        made = copy(("d", 1, 0, d), grad.at[1, r], grad.at[1, r], p, to)
+        start(made)
+        gsends[1].append(made)
+    agg = jnp.concatenate(aggs, axis=0)
+    gpre = jnp.concatenate(gpres, axis=0)
     gpre_parts = split(gpre)
-    gsends = []
-
-    def hidden_sends(c):
-        made_c = []
-        for d in range(m - 1, 0, -1):
-            to = lax.rem(r + d, m)
-            made = copy(("d", c, d), grad.at[c, r], grad.at[c, r], p, to)
-            made.start()
-            made_c.append(made)
-        gsends.append(made_c)
-
-    for c in range(HALVES):
-        columns = slice(c * cw, (c + 1) * cw)
-        grad[c, r] = dot3(gpre_parts, (wt[0][:, columns], wt[1][:, columns]))
-        if c == 0:
-            hidden_sends(0)
-    out[...] = jnp.where(pre > 0, pre, exped - 1.0)
 
     gw = dot3(split(agg.T), gpre_parts)
     gb = jnp.broadcast_to(jnp.sum(gpre, axis=0, keepdims=True), (8, width))
@@ -469,12 +499,8 @@
                 made_c.append(made)
         return made_c
 
-    for made in gsends[0]:
-        made.wait_send()
-    hidden_sends(1)
-    flush()
-    for made in gsends[1]:
-        started.append((made, always))
+    for made, cond in forward:
+        when(cond, made.wait_send)
     adjoint(0)
     made_z = weight_sums()
     adjoint(1)
@@ -518,7 +544,7 @@
     part, width = cotangent.shape
     cw = width // HALVES
     piece = width // n
-    copies = HALVES * (2 + 3 * (m - 1) + 4 * m) + 2 * (n - 1) + (m - 1)
+    copies = HALVES * (2 + 5 * (m - 1) + 4 * m) + 2 * (n - 1) + (m - 1)
     vmem = pl.BlockSpec(memory_space=pltpu.VMEM)
     shape = jax.ShapeDtypeStruct
     quarter = (HALVES, m, part, cw)

time: 67.7 us -> 68.1 us (level)
  no operation moved by 1% of the time
where the time goes in v5:
time: 68.1 us; the launch traced here: 67.9 us
  Pallas kernels  67.3 us (99%)
    pallas_call x1, Pallas kernels, fast_body(): pl.pallas_call(functools.partial(kernel, n, m), out_shape=(shape((part, w...  65.4 us
    pallas_call x1, Pallas kernels, fast_body(): pl.pallas_call(store_results, out_shape=[shape(value.shape, F32) for valu...  1.86 us

profile of v5, /device:TPU:1, one launch (start us, length us, event | category | flops | bytes accessed | tf_op | source)
XLA Modules:
  0.0 67.9 jit_solution(10771679858557287397)
XLA Ops:
  0.6 65.4 %shard_map.93 = (f32[128,256]{1,0:T(8,128)}, f32[128,256]{1,0:T(8,128)}, f32[256,256]{1,0:T(8,128)}, f32[1,256]{1,0:T(1,128)}) custom-call(f32[512,256]{1,0:T(8,128)} %feats.1, f32[4,4,128,128]{3,2,1,0:T(8,128)} %tiles_hbm.1, s32[4,4]{1,0:T(4,128)} %cols_hbm.1, f32[256,256]{1,0:T(8,128)} %weight_hbm.1, f32[1,256]{1,0:T(1,128)} %bitcast.2, f32[128,256]{1,0:T(8,128)} %cot_hbm.1), custom_call_target="tpu_custom_call" | custom-call | tf_op jit(solution)/shard_map/pallas_call | solution.py:551
  66.1 1.9 %shard_map.94 = (f32[128,256]{1,0:T(8,128)}, f32[128,256]{1,0:T(8,128)}, f32[256,256]{1,0:T(8,128)}, f32[1,256]{1,0:T(1,128)}) custom-call(f32[128,256]{1,0:T(8,128)} %get-tuple-element.12.refs_0_, f32[128,256]{1,0:T(8,128)} %get-tuple-element.13.refs_1_, f32[256,256]{1,0:T(8,128)} %get-tuple-element.14.refs_2_, f32[1,256]{1,0:T(1,128)} %get-tuple-element.15.refs_3_), custom_call_target="tpu_custom_call" | custom-call | tf_op jit(solution)/shard_map/pallas_call | solution.py:592

commit v6 on v5

--- a/solution.py
+++ b/solution.py
@@ -111,7 +111,9 @@
     def product(x, y):
         return jnp.dot(x, y, preferred_element_type=F32)
 
-    return product(a[0], b[0]) + (product(a[0], b[1]) + product(a[1], b[0]))
+    columns = b[0].shape[1]
+    pair = product(a[0], jnp.concatenate([b[0], b[1]], axis=1))
+    return pair[:, :columns] + (pair[:, columns:] + product(a[1], b[0]))
 
 
 def kernel(
@@ -314,6 +316,12 @@
     started.clear()
 
     gsends = [[] for _ in range(HALVES)]
+
+    def direct(d):
+        if d == m - 1:
+            return r != 0
+        return r != m - 1 if d == 1 else None
+
     aggs, gpres = [], []
     for s in range(ROW_PARTS):
         here = slice(s * some, (s + 1) * some)
@@ -332,16 +340,16 @@
                     to = lax.rem(r + d, m)
                     block = grad.at[c, r, row_part(s)]
                     made = copy(("d", c, s, d), block, block, p, to)
-                    start(made)
-                    gsends[c].append(made)
+                    start(made, direct(d))
+                    gsends[c].append((made, s, d))
         out[here] = jnp.where(pre > 0, pre, exped - 1.0)
         aggs.append(jnp.concatenate([early[here], late], axis=1))
         gpres.append(gpre)
     for d in range(m - 1, 0, -1):
         to = lax.rem(r + d, m)
         made = copy(("d", 1, 0, d), grad.at[1, r], grad.at[1, r], p, to)
-        start(made)
-        gsends[1].append(made)
+        start(made, direct(d))
+        gsends[1].append((made, None, d))
     agg = jnp.concatenate(aggs, axis=0)
     gpre = jnp.concatenate(gpres, axis=0)
     gpre_parts = split(gpre)
@@ -418,8 +426,17 @@
     plain_first = but(but(both(odd, moved), near_to), above)
 
     def adjoint(c):
-        for made in gsends[c]:
+        for made, s, d in gsends[c]:
+            if d != 2:
+                continue
             made.wait_recv()
+            for source, via, to, key in ((0, 2, 3, 3), (3, 1, 0, 1)):
+                block = grad.at[c, source] if s is None else grad.at[c, source, row_part(s)]
+                passed = copy(("d", c, s or 0, key), block, block, p, to)
+                start(passed, r == via)
+        for made, s, d in gsends[c]:
+            if d != 2:
+                made.wait_recv()
         g = split(grad[c].reshape(rows, cw))
         adj[1, c] = dot3((st_hi[rows:], st_lo[rows:]), g).reshape(m, part, cw)
         for d in order:

time: 68.1 us -> 66.9 us (0.982)
  Pallas kernels: 67.3 us -> 66.1 us
    pallas_call x1, Pallas kernels: 65.4 us -> 64.2 us  [fast_body(): pl.pallas_call(functools.partial(kernel, n, m), out_shape=(shape((part, w...]
where the time goes in v6:
time: 66.9 us; the launch traced here: 66.7 us
  Pallas kernels  66.1 us (99%)
    pallas_call x1, Pallas kernels, fast_body(): pl.pallas_call(functools.partial(kernel, n, m), out_shape=(shape((part, w...  64.2 us
    pallas_call x1, Pallas kernels, fast_body(): pl.pallas_call(store_results, out_shape=[shape(value.shape, F32) for valu...  1.86 us

profile of v6, /device:TPU:1, one launch (start us, length us, event | category | flops | bytes accessed | tf_op | source)
XLA Modules:
  0.0 66.7 jit_solution(2004828604356806661)
XLA Ops:
  0.6 64.2 %shard_map.93 = (f32[128,256]{1,0:T(8,128)}, f32[128,256]{1,0:T(8,128)}, f32[256,256]{1,0:T(8,128)}, f32[1,256]{1,0:T(1,128)}) custom-call(f32[512,256]{1,0:T(8,128)} %feats.1, f32[4,4,128,128]{3,2,1,0:T(8,128)} %tiles_hbm.1, s32[4,4]{1,0:T(4,128)} %cols_hbm.1, f32[256,256]{1,0:T(8,128)} %weight_hbm.1, f32[1,256]{1,0:T(1,128)} %bitcast.2, f32[128,256]{1,0:T(8,128)} %cot_hbm.1), custom_call_target="tpu_custom_call" | custom-call | tf_op jit(solution)/shard_map/pallas_call | solution.py:568
  64.8 1.9 %shard_map.94 = (f32[128,256]{1,0:T(8,128)}, f32[128,256]{1,0:T(8,128)}, f32[256,256]{1,0:T(8,128)}, f32[1,256]{1,0:T(1,128)}) custom-call(f32[128,256]{1,0:T(8,128)} %get-tuple-element.12.refs_0_, f32[128,256]{1,0:T(8,128)} %get-tuple-element.13.refs_1_, f32[256,256]{1,0:T(8,128)} %get-tuple-element.14.refs_2_, f32[1,256]{1,0:T(1,128)} %get-tuple-element.15.refs_3_), custom_call_target="tpu_custom_call" | custom-call | tf_op jit(solution)/shard_map/pallas_call | solution.py:609

commit v7 on v6

--- a/solution.py
+++ b/solution.py
@@ -120,7 +120,7 @@
     n, m, feats, tiles_hbm, cols_hbm, weight_hbm, bias_hbm, cot_hbm,
     out, gfeats, gweight, gbias,
     tiles, cols, weight, bias, cot,
-    xs, s_hi, s_lo, st_hi, st_lo, hpart, hrecv, grad, adj, fold, extra, total, frecv,
+    xs, s_hi, s_lo, st_hi, st_lo, hpart, hrecv, grad, adj, fold, total, frecv,
     gws, gwr, gwz, gfin, send_sem, recv_sem, load_sem,
 ):
     p, r = lax.axis_index("blk"), lax.axis_index("rep")
@@ -129,7 +129,6 @@
     part, width = cot.shape
     cw = width // HALVES
     piece = width // n
-    kind = lax.rem(p, 4)
     even = lax.rem(p, 2) == 0
     odd = jnp.logical_not(even)
     moved = r > 0
@@ -137,9 +136,6 @@
 
     def both(x, y):
         return jnp.logical_and(x, y)
-
-    def but(x, y):
-        return jnp.logical_and(x, jnp.logical_not(y))
 
     def when(cond, action):
         if cond is None:
@@ -147,10 +143,6 @@
         else:
             pl.when(cond)(action)
 
-    near_from = both(r == 1, kind == 2)
-    near_to = both(r == 1, kind == 1)
-    above = both(r == 3, kind == 3)
-    below = both(r == 2, kind == 2)
     nxt = lax.rem(p + 1, n)
     prv = lax.rem(p - 1 + n, n)
 
@@ -173,15 +165,7 @@
     for d in range(1, m):
         pl.semaphore_signal(barrier, inc=1, device_id={"blk": p, "rep": lax.rem(r + d, m)})
 
-    @pl.when(above)
-    def _():
-        pl.semaphore_signal(barrier, inc=1, device_id={"blk": prv, "rep": 2})
-
-    @pl.when(below)
-    def _():
-        pl.semaphore_signal(barrier, inc=1, device_id={"blk": nxt, "rep": 3})
-
-    pl.semaphore_wait(barrier, n + m - 2 + jnp.where(jnp.logical_or(above, below), 1, 0))
+    pl.semaphore_wait(barrier, n + m - 2)
 
     keys, started = {}, []
 
@@ -235,9 +219,6 @@
     for made in loads:
         made.wait()
     for s in range(2):
-        if s == 1:
-            flush()
-            send_features(1)
         owner = lax.rem(p - 2 * r - s + 2 * n, n)
         for b in range(blocks):
             name = owner * blocks + b
@@ -252,6 +233,9 @@
                 high, low = split(tile.T)
                 st_hi[at, i * size : (i + 1) * size] = high
                 st_lo[at, i * size : (i + 1) * size] = low
+
+    flush()
+    send_features(1)
 
     def take_first(c):
         @pl.when(moved)
@@ -411,19 +395,9 @@
         b = place(d)
         return copy(("f", c, d), adj.at[1, c, b], fold.at[c, b], blk, r)
 
-    def to_near(c, d):
-        b = place(d)
-        return copy(("g", c, d), adj.at[0, c, b], extra.at[c, b], nxt, r)
-
-    def to_above(c, b):
-        return copy(("h", c, b), adj.at[1, c, b], extra.at[c, b], nxt, r + 1)
-
     def to_total(c, d):
         b = place(d)
         return copy(("k", c, d), adj.at[0, c, b], total.at[c, b], back, r)
-
-    plain_second = but(but(even, below), near_from)
-    plain_first = but(but(both(odd, moved), near_to), above)
 
     def adjoint(c):
         for made, s, d in gsends[c]:
@@ -441,13 +415,10 @@
         adj[1, c] = dot3((st_hi[rows:], st_lo[rows:]), g).reshape(m, part, cw)
         for d in order:
             start(to_fold(c, d, prv), odd)
-            start(to_fold(c, d, before), plain_second)
-        for b in range(m):
-            start(to_above(c, b), below)
+            start(to_fold(c, d, before), even)
         adj[0, c] = dot3((st_hi[:rows], st_lo[:rows]), g).reshape(m, part, cw)
         for d in order:
-            start(to_near(c, d), near_to)
-            start(to_total(c, d), plain_first)
+            start(to_total(c, d), both(odd, moved))
 
         @pl.when(even)
         def _():
@@ -457,36 +428,16 @@
                 adj[0, c, b] = adj[0, c, b] + fold[c, b]
                 pl.when(moved)(to_total(c, d).start)
 
-        @pl.when(above)
-        def _():
-            for d in order:
-                b = (3 + d) % m
-                to_above(c, b).wait_recv()
-                adj[0, c, b] = adj[0, c, b] + extra[c, b]
-                to_total(c, d).start()
-
-        @pl.when(near_from)
-        def _():
-            for d in order:
-                b = place(d)
-                to_near(c, d).wait_recv()
-                adj[1, c, b] = adj[1, c, b] + extra[c, b]
-                to_fold(c, d, before).start()
-
         for d in order:
             started.append((to_total(c, d), both(even, moved)))
-            started.append((to_total(c, d), above))
-            started.append((to_fold(c, d, before), near_from))
-
-    from_total = but(moved, both(r == 1, kind == 3))
-    from_fold = but(odd, both(r == 2, kind == 1))
+
 
     def adjoint_reduce(c):
         made_c = []
         for d in order:
             b = place(d)
 
-            @pl.when(from_total)
+            @pl.when(moved)
             def _():
                 to_total(c, d).wait_recv()
 
@@ -494,21 +445,10 @@
             def _():
                 total[c, b] = adj[0, c, b]
 
-            @pl.when(from_fold)
+            @pl.when(odd)
             def _():
                 to_fold(c, d, prv).wait_recv()
-
-                @pl.when(from_total)
-                def _():
-                    total[c, b] = total[c, b] + fold[c, b]
-
-                @pl.when(r == 0)
-                def _():
-                    total[c, b] = total[c, b] + fold[c, b]
-
-                @pl.when(both(r == 1, kind == 3))
-                def _():
-                    total[c, b] = fold[c, b]
+                total[c, b] = total[c, b] + fold[c, b]
 
             if d:
                 made = copy(("l", c, d), total.at[c, b], frecv.at[c, d - 1], p, b)
@@ -592,7 +532,6 @@
             pltpu.VMEM((2,) + quarter, F32),
             pltpu.VMEM(quarter, F32),
             pltpu.VMEM(quarter, F32),
-            pltpu.VMEM(quarter, F32),
             pltpu.VMEM((HALVES, m - 1, part, cw), F32),
             pltpu.VMEM((n, piece + 8, width), F32),
             pltpu.VMEM((n, piece + 8, width), F32),

time: 66.9 us -> 62.1 us (0.928)
  the two profiles are of different devices: /device:TPU:1 before, /device:TPU:0 now
where the time goes in v7:
time: 62.1 us; the launch traced here: 62 us
  Pallas kernels  61.3 us (99%)
  between operations  0.64 us (1%)
    pallas_call x1, Pallas kernels, fast_body(): pl.pallas_call(functools.partial(kernel, n, m), out_shape=(shape((part, w...  59.5 us
    pallas_call x1, Pallas kernels, fast_body(): pl.pallas_call(store_results, out_shape=[shape(value.shape, F32) for valu...  1.86 us

profile of v7, /device:TPU:0, one launch (start us, length us, event | category | flops | bytes accessed | tf_op | source)
XLA Modules:
  0.0 62.0 jit_solution(143064181373968086)
XLA Ops:
  0.6 59.5 %shard_map.93 = (f32[128,256]{1,0:T(8,128)}, f32[128,256]{1,0:T(8,128)}, f32[256,256]{1,0:T(8,128)}, f32[1,256]{1,0:T(1,128)}) custom-call(f32[512,256]{1,0:T(8,128)} %feats.1, f32[4,4,128,128]{3,2,1,0:T(8,128)} %tiles_hbm.1, s32[4,4]{1,0:T(4,128)} %cols_hbm.1, f32[256,256]{1,0:T(8,128)} %weight_hbm.1, f32[1,256]{1,0:T(1,128)} %bitcast.2, f32[128,256]{1,0:T(8,128)} %cot_hbm.1), custom_call_target="tpu_custom_call" | custom-call | tf_op jit(solution)/shard_map/pallas_call | solution.py:508
  60.1 1.9 %shard_map.94 = (f32[128,256]{1,0:T(8,128)}, f32[128,256]{1,0:T(8,128)}, f32[256,256]{1,0:T(8,128)}, f32[1,256]{1,0:T(1,128)}) custom-call(f32[128,256]{1,0:T(8,128)} %get-tuple-element.12.refs_0_, f32[128,256]{1,0:T(8,128)} %get-tuple-element.13.refs_1_, f32[256,256]{1,0:T(8,128)} %get-tuple-element.14.refs_2_, f32[1,256]{1,0:T(1,128)} %get-tuple-element.15.refs_3_), custom_call_target="tpu_custom_call" | custom-call | tf_op jit(solution)/shard_map/pallas_call | solution.py:548

commit v8 on v7

--- a/solution.py
+++ b/solution.py
@@ -300,12 +300,6 @@
     started.clear()
 
     gsends = [[] for _ in range(HALVES)]
-
-    def direct(d):
-        if d == m - 1:
-            return r != 0
-        return r != m - 1 if d == 1 else None
-
     aggs, gpres = [], []
     for s in range(ROW_PARTS):
         here = slice(s * some, (s + 1) * some)
@@ -324,16 +318,16 @@
                     to = lax.rem(r + d, m)
                     block = grad.at[c, r, row_part(s)]
                     made = copy(("d", c, s, d), block, block, p, to)
-                    start(made, direct(d))
-                    gsends[c].append((made, s, d))
+                    start(made)
+                    gsends[c].append(made)
         out[here] = jnp.where(pre > 0, pre, exped - 1.0)
         aggs.append(jnp.concatenate([early[here], late], axis=1))
         gpres.append(gpre)
     for d in range(m - 1, 0, -1):
         to = lax.rem(r + d, m)
         made = copy(("d", 1, 0, d), grad.at[1, r], grad.at[1, r], p, to)
-        start(made, direct(d))
-        gsends[1].append((made, None, d))
+        start(made)
+        gsends[1].append(made)
     agg = jnp.concatenate(aggs, axis=0)
     gpre = jnp.concatenate(gpres, axis=0)
     gpre_parts = split(gpre)
@@ -400,17 +394,8 @@
         return copy(("k", c, d), adj.at[0, c, b], total.at[c, b], back, r)
 
     def adjoint(c):
-        for made, s, d in gsends[c]:
-            if d != 2:
-                continue
+        for made in gsends[c]:
             made.wait_recv()
-            for source, via, to, key in ((0, 2, 3, 3), (3, 1, 0, 1)):
-                block = grad.at[c, source] if s is None else grad.at[c, source, row_part(s)]
-                passed = copy(("d", c, s or 0, key), block, block, p, to)
-                start(passed, r == via)
-        for made, s, d in gsends[c]:
-            if d != 2:
-                made.wait_recv()
         g = split(grad[c].reshape(rows, cw))
         adj[1, c] = dot3((st_hi[rows:], st_lo[rows:]), g).reshape(m, part, cw)
         for d in order:
@@ -431,7 +416,6 @@
         for d in order:
             started.append((to_total(c, d), both(even, moved)))
 
-
     def adjoint_reduce(c):
         made_c = []
         for d in order:
@@ -464,16 +448,15 @@
     lsends = [adjoint_reduce(0)]
     made_n = weight_gather(made_z)
     lsends.append(adjoint_reduce(1))
-    flush()
     for c in range(HALVES):
         if c == 1:
+            flush()
             for made in made_n:
                 made.wait_recv()
             gweight[...] = gfin[...].reshape(width, width)
         for made in lsends[c]:
             made.wait_recv()
         gfeats[:, half(c)] = total[c, r] + ((frecv[c, 0] + frecv[c, 1]) + frecv[c, 2])
-    flush()
 
 
 def store_results(*refs):

time: 62.1 us -> 62.5 us (level)
  the two profiles are of different devices: /device:TPU:0 before, /device:TPU:4 now
where the time goes in v8:
time: 62.5 us; the launch traced here: 62.3 us
  Pallas kernels  61.7 us (99%)
  between operations  0.64 us (1%)
    pallas_call x1, Pallas kernels, fast_body(): pl.pallas_call(functools.partial(kernel, n, m), out_shape=(shape((part, w...  59.8 us
    pallas_call x1, Pallas kernels, fast_body(): pl.pallas_call(store_results, out_shape=[shape(value.shape, F32) for valu...  1.86 us

profile of v8, /device:TPU:4, one launch (start us, length us, event | category | flops | bytes accessed | tf_op | source)
XLA Modules:
  0.0 62.3 jit_solution(8994918505258697475)
XLA Ops:
  0.6 59.8 %shard_map.93 = (f32[128,256]{1,0:T(8,128)}, f32[128,256]{1,0:T(8,128)}, f32[256,256]{1,0:T(8,128)}, f32[1,256]{1,0:T(1,128)}) custom-call(f32[512,256]{1,0:T(8,128)} %feats.1, f32[4,4,128,128]{3,2,1,0:T(8,128)} %tiles_hbm.1, s32[4,4]{1,0:T(4,128)} %cols_hbm.1, f32[256,256]{1,0:T(8,128)} %weight_hbm.1, f32[1,256]{1,0:T(1,128)} %bitcast.2, f32[128,256]{1,0:T(8,128)} %cot_hbm.1), custom_call_target="tpu_custom_call" | custom-call | tf_op jit(solution)/shard_map/pallas_call | solution.py:491
  60.5 1.9 %shard_map.94 = (f32[128,256]{1,0:T(8,128)}, f32[128,256]{1,0:T(8,128)}, f32[256,256]{1,0:T(8,128)}, f32[1,256]{1,0:T(1,128)}) custom-call(f32[128,256]{1,0:T(8,128)} %get-tuple-element.12.refs_0_, f32[128,256]{1,0:T(8,128)} %get-tuple-element.13.refs_1_, f32[256,256]{1,0:T(8,128)} %get-tuple-element.14.refs_2_, f32[1,256]{1,0:T(1,128)} %get-tuple-element.15.refs_3_), custom_call_target="tpu_custom_call" | custom-call | tf_op jit(solution)/shard_map/pallas_call | solution.py:531
